TPU v7x, 128 devices: a whole 4x4x4 slice. The times are simulated.
128 devices in a mesh: gx: 8 (over y, core), gy: 16 (over z, x).
Axes of the slice: x: 4, y: 4, z: 4, core: 2. Of those that a mesh axis runs over, the one named last changes fastest.
Arguments:
- molar_density_logs: float32 [1024, 53, 2048], P('gx', None, 'gy'), may hold values from -2.5 to -0.5
- scaled_thermal_state: float32 [1024, 2048], P('gx', 'gy'), may hold values from 1.5 to 3
- spreading_rate: float32 [1024, 2048], P('gx', 'gy'), may hold values from 0.2 to 2
- tile_burning_load: int32 [1024, 16], P('gx', 'gy'), may hold values from 0 to 1, as said below
- input_multipliers: int32 [325, 53], replicated, may hold values from 0 to 2, as said below
- output_multipliers: int32 [325, 53], replicated, may hold values from 0 to 2, as said below
- arrhenius_prefactor_logs: float32 [325], replicated, may hold values from 0 to 2
- arrhenius_barrier: float32 [325], replicated, may hold values from 0.5 to 4
- balance_ratio_logs: float32 [325], replicated, may hold values from -1 to 1
- enthalpy_yield: float32 [325], replicated, may hold values from -3 to 3
Outputs:
- new_conc: float32 [1024, 53, 2048], P('gx', None, 'gy')
- new_temp: float32 [1024, 2048], P('gx', 'gy')
Inputs may be any that keep to these rules, and one draw needn't show every extreme that they name: `tile_burning_load`: among the 2048 blocks of each group of 128 rows that starts at a multiple of 128, exactly 1024 have cost 1, and in every such group all 128 blocks of some column have cost 1. `input_multipliers`: each row's entries add up to 1 or 2; some entry is 2. `output_multipliers`: each row's entries add up to 1 or 2; some entry is 2.
All inputs are finite; a program needn't handle non-finite values.
Results may differ from a plain program's by a relative error of at most 0.0001.
Values sent between devices are 32-bit elements; how exact they have to be, the bound alone decides.
A program may use at most 192 MiB of HBM per device.

v0:
```python
import jax
import jax.numpy as jnp
from jax import lax
from jax.experimental import pallas as pl
from jax.experimental.pallas import tpu as pltpu
from jax.sharding import PartitionSpec as P

SUBSTEPS = 4
TIME_STEP = 0.01
DIFFUSION_NUMBER = 0.1
LOG2E = 1.4426950408889634
LN2 = 0.6931471805599453

TILE = 8
CHUNK = 16
AHEAD = 4
SLOTS = 64
FIELD_ROWS = 56
BLOCK = 6
UP, DOWN, LEFT, RIGHT = range(4)

BF16 = jnp.bfloat16
F32 = jnp.float32


def split_pair(x):
    high = x.astype(BF16).astype(F32)
    return high, x - high


def split_three(x):
    first = x.astype(BF16).astype(F32)
    rest = x - first
    second = rest.astype(BF16).astype(F32)
    return first, second, rest - second


def fill_tables(
    forward_ref, backward_ref, law_refs, exponent_table, sum_table, line, stage
):
    species, laws = forward_ref.shape
    total = exponent_table.shape[0]
    padded = total // 2
    wide = stage.shape[1]
    stage[...] = jnp.zeros_like(stage)
    line[...] = jnp.zeros_like(line)
    for index, ref in enumerate(law_refs):
        line[index : index + 1, 0:laws] = ref[...].reshape(1, laws)
    prefactor, barrier, balance, heat = (line[index : index + 1] for index in range(4))
    b1, b2, b3 = split_three((-LOG2E * LOG2E) * barrier)

    def table(table_ref, constant):
        stage[0:species, 0:laws] = table_ref[...].astype(F32)
        stage[SLOTS : SLOTS + species, 0:laws] = table_ref[...].astype(F32)
        for index, piece in enumerate((b1, b2, b3) + split_three(LOG2E * constant)):
            stage[species + index : species + index + 1] = piece
        for index, piece in enumerate((b1, b2)):
            at = SLOTS + species + index
            stage[at : at + 1] = piece
        return stage[...].T[:padded]

    first = table(forward_ref, prefactor)
    second = table(backward_ref, prefactor - balance)
    pairs = [half.reshape(padded // 8, 1, 8, 2 * SLOTS) for half in (first, second)]
    pairs = jnp.concatenate(pairs, axis=1).reshape(total, 2 * SLOTS)
    exponent_table[...] = pairs.astype(BF16)

    stage[...] = jnp.zeros_like(stage)
    stage[0:species, 0:laws] = (backward_ref[...] - forward_ref[...]).astype(F32)
    high, low = split_pair(heat)
    stage[species : species + 1] = high
    stage[species + 8 : species + 9] = low
    law = lax.broadcasted_iota(jnp.int32, (wide, total), 0)
    place = lax.broadcasted_iota(jnp.int32, (wide, total), 1)
    chosen = jnp.where(law == (place // 16) * 8 + place % 8, 1.0, 0.0).astype(BF16)
    spread = jnp.dot(stage[0:SLOTS].astype(BF16), chosen, preferred_element_type=F32)
    sum_table[...] = spread.astype(BF16)


def chemistry_kernel(
    logs_ref,
    temper_ref,
    spread_ref,
    load_input,
    forward_input,
    backward_input,
    prefactor_input,
    barrier_input,
    balance_input,
    heat_input,
    state_ref,
    halo_ref,
    cells_ref,
    load_ref,
    forward_ref,
    backward_ref,
    prefactor_ref,
    barrier_ref,
    balance_ref,
    heat_ref,
    edges,
    halos,
    sides,
    exponent_table,
    sum_table,
    line,
    stage,
    fields_a,
    fields_b,
    operand_a,
    operand_b,
    net_a,
    net_b,
    small_sem,
    plane_sem,
    in_sem,
    out_sem,
    halo_sem,
    send_sem,
    recv_sem,
):
    species, rows, width = logs_ref.shape
    tiles, chunks = rows // TILE, rows // CHUNK
    share = CHUNK // TILE
    cells = CHUNK * width
    laws = exponent_table.shape[0] // 2
    gx, gy = lax.axis_index("gx"), lax.axis_index("gy")
    nx, ny = lax.axis_size("gx"), lax.axis_size("gy")
    up = (lax.rem(gx + nx - 1, nx), gy)
    down = (lax.rem(gx + 1, nx), gy)
    left = (gx, lax.rem(gy + ny - 1, ny))
    right = (gx, lax.rem(gy + 1, ny))

    def fetch(tile):
        at = pl.ds(pl.multiple_of(tile * TILE, TILE), TILE)
        target = cells_ref.at[tile, pl.ds(0, species)]
        return pltpu.make_async_copy(logs_ref.at[:, at], target, in_sem.at[tile])

    def spread_out(plane_ref, place, sem):
        target = cells_ref.at[pl.ds(0, tiles), place]
        return pltpu.make_async_copy(plane_ref.reshape(tiles, TILE, width), target, sem)

    def flush(tile):
        at = pl.ds(pl.multiple_of(tile * TILE, TILE), TILE)
        return pltpu.make_async_copy(cells_ref.at[tile], state_ref.at[:, at], out_sem.at[tile])

    def leave(chunk):
        for index in range(share):
            flush(chunk * share + index).start()

    def sends():
        copies = []
        for place, device in ((UP, down), (DOWN, up), (LEFT, right), (RIGHT, left)):
            copies.append(
                pltpu.make_async_remote_copy(
                    src_ref=edges.at[place],
                    dst_ref=halos.at[place],
                    send_sem=send_sem.at[place],
                    recv_sem=recv_sem.at[place],
                    device_id=device,
                    device_id_type=pl.DeviceIdType.MESH,
                )
            )
        return copies

    pairs_of = (
        (load_input, load_ref),
        (forward_input, forward_ref),
        (backward_input, backward_ref),
        (prefactor_input, prefactor_ref),
        (barrier_input, barrier_ref),
        (balance_input, balance_ref),
        (heat_input, heat_ref),
    )
    smalls = [
        pltpu.make_async_copy(source, target, small_sem.at[index])
        for index, (source, target) in enumerate(pairs_of)
    ]
    smalls.append(spread_out(temper_ref, species, plane_sem.at[0]))
    smalls.append(spread_out(spread_ref, species + 1, plane_sem.at[1]))
    fetch(0).start()
    for copy in smalls:
        copy.start()

    @pl.loop(1, tiles)
    def _(tile):
        fetch(tile).start()

    barrier = pltpu.get_barrier_semaphore()
    for neighbour in (up, down, left, right):
        pl.semaphore_signal(
            barrier, inc=1, device_id=neighbour, device_id_type=pl.DeviceIdType.MESH
        )

    for copy in smalls:
        copy.wait()
    steps = jnp.where(load_ref[...] > 0, TIME_STEP * LOG2E, 0.0).astype(F32)
    steps = jnp.broadcast_to(steps, (rows, width)).T
    for tile in range(tiles):
        cells_ref[tile, species + 2] = steps[tile * TILE : (tile + 1) * TILE]
    fill_tables(
        forward_ref,
        backward_ref,
        (prefactor_ref, barrier_ref, balance_ref, heat_ref),
        exponent_table,
        sum_table,
        line,
        stage,
    )

    sides[...] = jnp.zeros_like(sides)
    cells_ref[tiles:] = jnp.zeros((share,) + cells_ref.shape[1:], F32)
    split = FIELD_ROWS - 8
    lane = lax.broadcasted_iota(jnp.int32, (FIELD_ROWS, width), 1)
    flat = cells_ref.reshape((tiles + share) * FIELD_ROWS * TILE, width)

    def row_of(chunk, row):
        tile = chunk * share + row // TILE
        return pl.ds(tile * (FIELD_ROWS * TILE) + row % TILE, FIELD_ROWS, stride=TILE)

    def slots(like):
        return lax.broadcasted_iota(jnp.int32, (8, like.shape[1]), 0)

    def operand_of(body, end):
        slot = slots(end)
        inverse = 1.0 / end[species - split : species - split + 1]
        inverse = jnp.broadcast_to(inverse, end.shape)
        end = jnp.where(slot < species - split, end, inverse)
        high, low = split_pair(jnp.concatenate([body, end], axis=0))
        ones = jnp.where(slot < 3, 1.0, 0.0).astype(F32)
        parts = [high, ones, low, jnp.zeros_like(ones)]
        return jnp.concatenate(parts, axis=0).astype(BF16)

    def load(fields, fields_ref, operand_ref):
        body, end = fields[:split] * LOG2E, fields[split:]
        end = jnp.where(slots(end) == 7, end, end * LOG2E)
        fields_ref[0:split] = body
        fields_ref[split:FIELD_ROWS] = end
        operand_ref[...] = operand_of(body, end)

    def chunk_of(chunk):
        return jnp.concatenate([flat[row_of(chunk, row)] for row in range(CHUNK)], axis=1)

    def rates(operand_ref, net_ref):
        powers = jnp.dot(exponent_table[...], operand_ref[...], preferred_element_type=F32)
        count = powers.shape[1]
        powers = powers.reshape(laws // 8, 2, 8, count)
        net = jnp.exp2(powers[:, 0]) - jnp.exp2(powers[:, 1])
        high, low = split_pair(net)
        pieces = jnp.concatenate([high[:, None], low[:, None]], axis=1)
        net_ref[...] = pieces.reshape(2 * laws, count).astype(BF16)

    def advance(net_ref, fields_ref):
        change = jnp.dot(sum_table[...], net_ref[...], preferred_element_type=F32)
        end_change = change[split:FIELD_ROWS] + change[FIELD_ROWS:]
        body, end = fields_ref[0:split], fields_ref[split:FIELD_ROWS]
        slot = slots(end)
        step = end[7:8]
        gain = jnp.where(
            slot < species - split,
            jnp.exp2(-end),
            jnp.where(slot == species - split, 1.0, 0.0),
        )
        body = body + step * (change[:split] * jnp.exp2(-body))
        end = end + step * (end_change * gain)
        return body, end

    def renew(net_ref, fields_ref, operand_ref):
        body, end = advance(net_ref, fields_ref)
        fields_ref[0:split] = body
        fields_ref[split:FIELD_ROWS] = end
        operand_ref[...] = operand_of(body, end)

    def finish(chunk, body, end):
        fields = jnp.concatenate([body, end], axis=0) * LN2
        for row in range(CHUNK):
            flat[row_of(chunk, row)] = fields[:, row * width : (row + 1) * width]

    def collect(chunk):
        base = chunk * CHUNK
        first = jnp.zeros((FIELD_ROWS, width), F32)
        last = jnp.zeros((FIELD_ROWS, width), F32)
        for row in range(CHUNK):
            part = flat[row_of(chunk, row)]
            first = jnp.where(lane == row, pltpu.roll(part, row, 1), first)
            last = jnp.where(lane == row, pltpu.roll(part, row + 1, 1), last)
        mine = (lane >= base) & (lane < base + CHUNK)
        turn = base % width
        sides[0] = jnp.where(mine, pltpu.roll(first, turn, 1), sides[0])
        sides[1] = jnp.where(mine, pltpu.roll(last, turn, 1), sides[1])

    for tile in range(share):
        fetch(tile).wait()
    collect(0)
    edges[DOWN] = flat[row_of(0, 0)]
    load(chunk_of(0), fields_a, operand_a)
    fields_b[...] = jnp.ones_like(fields_b)
    net_b[...] = jnp.zeros_like(net_b)
    pairs = chunks // 2
    gathered = chunks // AHEAD

    @pl.loop(0, pairs)
    def _(pair):
        a, b = 2 * pair, 2 * pair + 1

        @pl.when(pair == 0)
        def _():
            for tile in range(share, 3 * share):
                fetch(tile).wait()

        @pl.when(pair == 1)
        def _():
            @pl.loop(3 * share, tiles)
            def _(tile):
                fetch(tile).wait()

        @pl.when(pair == gathered + 1)
        def _():
            edges[RIGHT] = sides[0]
            edges[LEFT] = sides[1]
            edges[UP] = flat[row_of(chunks - 1, CHUNK - 1)]
            pl.semaphore_wait(barrier, 4)
            for copy in sends():
                copy.start()

        @pl.when(pair > 0)
        def _():
            leave(a - 2)

        @pl.when(pair > 1)
        def _():
            leave(b - 4)

        collects = (pair > 0) & (pair <= gathered)
        for index in range(AHEAD):
            collect(jnp.where(collects, (pair - 1) * AHEAD + 1 + index, chunks))

        for substep in range(SUBSTEPS):
            rates(operand_a, net_a)
            if substep == 0:
                finish(jnp.where(pair == 0, chunks, b - 2), *advance(net_b, fields_b))
                load(chunk_of(b), fields_b, operand_b)
            else:
                renew(net_b, fields_b, operand_b)
            rates(operand_b, net_b)
            if substep == SUBSTEPS - 1:
                finish(a, *advance(net_a, fields_a))
                load(chunk_of(jnp.minimum(a + 2, chunks - 1)), fields_a, operand_a)
            else:
                renew(net_a, fields_a, operand_a)

    leave(chunks - 3)
    leave(chunks - 2)
    for copy in sends():
        copy.wait()
    finish(chunks - 1, *advance(net_b, fields_b))
    count = 4 * width
    fields_h, operand_h, net_h = (
        ref.at[:, pl.ds(0, count)] for ref in (fields_a, operand_a, net_a)
    )
    load(jnp.concatenate([halos[place] for place in range(4)], axis=1), fields_h, operand_h)
    for _ in range(SUBSTEPS):
        rates(operand_h, net_h)
        renew(net_h, fields_h, operand_h)
    leave(chunks - 1)
    for place in range(4):
        edges[place] = fields_h[:, place * width : (place + 1) * width] * LN2
    copy = pltpu.make_async_copy(edges, halo_ref, halo_sem)
    copy.start()

    @pl.loop(0, tiles)
    def _(tile):
        flush(tile).wait()

    copy.wait()


def transport_kernel(
    state_ref,
    spread_input,
    halo_input,
    conc_ref,
    temp_ref,
    spread_ref,
    halo_ref,
    old,
    new,
    gains,
    sides,
    sheet,
    small_sem,
    in_sem,
    out_sem,
    temp_sem,
):
    species, rows, width = conc_ref.shape
    blocks = (species + 1) // BLOCK
    row = lax.broadcasted_iota(jnp.int32, (rows, width), 0)
    lane = lax.broadcasted_iota(jnp.int32, (rows, width), 1)

    def fetch(block):
        at = pl.ds(block * BLOCK, BLOCK)
        return pltpu.make_async_copy(state_ref.at[at], old.at[at], in_sem.at[block])

    def flush(block, count):
        at = pl.ds(block * BLOCK, count)
        return pltpu.make_async_copy(new.at[at], conc_ref.at[at], out_sem.at[block])

    def flush_temper():
        return pltpu.make_async_copy(new.at[species], temp_ref, temp_sem)

    smalls = [
        pltpu.make_async_copy(halo_input, halo_ref, small_sem.at[0]),
        pltpu.make_async_copy(spread_input, spread_ref, small_sem.at[1]),
    ]
    for copy in smalls:
        copy.start()

    @pl.loop(0, blocks)
    def _(block):
        fetch(block).start()

    for copy in smalls:
        copy.wait()

    def around(here, component):
        north = jnp.where(row == 0, halo_ref[UP, component], pltpu.roll(here, 1, 0))
        south = jnp.where(
            row == rows - 1, halo_ref[DOWN, component], pltpu.roll(here, rows - 1, 0)
        )
        side = pltpu.roll(sides[...], width - 1 - 2 * component, 1)
        west = jnp.where(lane == 0, side, pltpu.roll(here, 1, 1))
        east = jnp.where(lane == width - 1, side, pltpu.roll(here, width - 1, 1))
        return north, south, west, east

    sheet[...] = jnp.zeros_like(sheet)
    sheet[pl.ds(0, FIELD_ROWS, stride=2)] = halo_ref[RIGHT]
    sheet[pl.ds(1, FIELD_ROWS, stride=2)] = halo_ref[LEFT]
    sides[...] = sheet[...].T
    here = spread_ref[...]
    rest = jnp.ones_like(here)
    for index, near in enumerate(around(here, FIELD_ROWS - 2)):
        gain = (0.5 * DIFFUSION_NUMBER) * (here + near)
        gains[index] = gain
        rest = rest - gain
    gains[4] = rest

    @pl.loop(0, blocks)
    def _(block):
        fetch(block).wait()
        for index in range(BLOCK):
            component = block * BLOCK + index
            here = old[component]
            total = gains[4] * here
            for which, near in enumerate(around(here, component)):
                total = total + gains[which] * near
            new[component] = total

        @pl.when(block < blocks - 1)
        def _():
            flush(block, BLOCK).start()

    flush(blocks - 1, BLOCK - 1).start()
    flush_temper().start()

    @pl.loop(0, blocks - 1)
    def _(block):
        flush(block, BLOCK).wait()

    flush(blocks - 1, BLOCK - 1).wait()
    flush_temper().wait()


def per_device(
    molar_density_logs,
    scaled_thermal_state,
    spreading_rate,
    tile_burning_load,
    input_multipliers,
    output_multipliers,
    arrhenius_prefactor_logs,
    arrhenius_barrier,
    balance_ratio_logs,
    enthalpy_yield,
):
    rows, species, width = molar_density_logs.shape
    laws = input_multipliers.shape[0]
    padded = -(-laws // 8) * 8
    wide = -(-laws // 128) * 128
    tiles = rows // TILE
    cells = CHUNK * width
    anywhere = pl.BlockSpec(memory_space=pl.ANY)
    state, halo = pl.pallas_call(
        chemistry_kernel,
        out_shape=(
            jax.ShapeDtypeStruct((FIELD_ROWS, rows, width), F32),
            jax.ShapeDtypeStruct((4, FIELD_ROWS, width), F32),
        ),
        in_specs=[anywhere] * 10,
        out_specs=(anywhere,) * 2,
        scratch_shapes=[
            pltpu.VMEM((tiles + CHUNK // TILE, FIELD_ROWS, TILE, width), F32),
            pltpu.VMEM((1, rows), jnp.int32),
            pltpu.VMEM((species, laws), jnp.int32),
            pltpu.VMEM((species, laws), jnp.int32),
            pltpu.VMEM((laws,), F32),
            pltpu.VMEM((laws,), F32),
            pltpu.VMEM((laws,), F32),
            pltpu.VMEM((laws,), F32),
            pltpu.VMEM((4, FIELD_ROWS, width), F32),
            pltpu.VMEM((4, FIELD_ROWS, width), F32),
            pltpu.VMEM((2, FIELD_ROWS, width), F32),
            pltpu.VMEM((2 * padded, 2 * SLOTS), BF16),
            pltpu.VMEM((SLOTS, 2 * padded), BF16),
            pltpu.VMEM((8, wide), F32),
            pltpu.VMEM((2 * SLOTS, wide), F32),
            pltpu.VMEM((FIELD_ROWS, cells), F32),
            pltpu.VMEM((FIELD_ROWS, cells), F32),
            pltpu.VMEM((2 * SLOTS, cells), BF16),
            pltpu.VMEM((2 * SLOTS, cells), BF16),
            pltpu.VMEM((2 * padded, cells), BF16),
            pltpu.VMEM((2 * padded, cells), BF16),
            pltpu.SemaphoreType.DMA((7,)),
            pltpu.SemaphoreType.DMA((2,)),
            pltpu.SemaphoreType.DMA((tiles,)),
            pltpu.SemaphoreType.DMA((tiles,)),
            pltpu.SemaphoreType.DMA(()),
            pltpu.SemaphoreType.DMA((4,)),
            pltpu.SemaphoreType.DMA((4,)),
        ],
        compiler_params=pltpu.CompilerParams(
            collective_id=0, has_side_effects=True, vmem_limit_bytes=60 * 2**20
        ),
        name="chemistry",
    )(
        jnp.transpose(molar_density_logs, (1, 0, 2)),
        scaled_thermal_state,
        spreading_rate,
        tile_burning_load.reshape(1, rows),
        input_multipliers.T,
        output_multipliers.T,
        arrhenius_prefactor_logs,
        arrhenius_barrier,
        balance_ratio_logs,
        enthalpy_yield,
    )

    blocks = (species + 1) // BLOCK
    conc, temp = pl.pallas_call(
        transport_kernel,
        out_shape=(
            jax.ShapeDtypeStruct((species, rows, width), F32),
            jax.ShapeDtypeStruct((rows, width), F32),
        ),
        in_specs=[anywhere] * 3,
        out_specs=(anywhere, anywhere),
        scratch_shapes=[
            pltpu.VMEM((rows, width), F32),
            pltpu.VMEM((4, FIELD_ROWS, width), F32),
            pltpu.VMEM((species + 1, rows, width), F32),
            pltpu.VMEM((species + 1, rows, width), F32),
            pltpu.VMEM((5, rows, width), F32),
            pltpu.VMEM((rows, width), F32),
            pltpu.VMEM((width, rows), F32),
            pltpu.SemaphoreType.DMA((2,)),
            pltpu.SemaphoreType.DMA((blocks,)),
            pltpu.SemaphoreType.DMA((blocks,)),
            pltpu.SemaphoreType.DMA(()),
        ],
        compiler_params=pltpu.CompilerParams(vmem_limit_bytes=60 * 2**20),
        name="transport",
    )(state, spreading_rate, halo)
    return jnp.transpose(conc, (1, 0, 2)), temp


def solution(mesh):
    placed = (
        P("gx", None, "gy"),
        P("gx", "gy"),
        P("gx", "gy"),
        P("gx", "gy"),
        P(),
        P(),
        P(),
        P(),
        P(),
        P(),
    )
    return jax.shard_map(
        per_device,
        mesh=mesh,
        in_specs=placed,
        out_specs=(P("gx", None, "gy"), P("gx", "gy")),
        check_vma=False,
    )
```

profile of v0, /device:TPU:0, one launch (start us, length us, event | category | flops | bytes accessed | tf_op | source)
XLA Modules:
  0.0 54.6 jit_solution(279482790689455925)
XLA Ops:
  0.6 48.5 %chemistry.1 = (f32[56,128,128]{2,1,0:T(8,128)}, f32[4,56,128]{2,1,0:T(8,128)}) custom-call(f32[53,128,128]{2,1,0:T(8,128)} %bitcast.5, f32[128,128]{1,0:T(8,128)} %temper_ref.1, f32[128,128]{1,0:T(8,128)} %spread_input.1, s32[1,128]{1,0:T(1,128)} %bitcast.8, s32[53,325]{1,0:T(8,128)} %bitcast.6, s32[53,325]{1,0:T(8,128)} %bitcast.7, f32[325]{0:T(512)} %prefactor_input.1, ...), custom_call_target="tpu_custom_call" | custom-call | tf_op jit(solution)/shard_map/chemistry/pallas_call | solution.py:493
  49.2 5.4 %transport.1 = (f32[53,128,128]{2,1,0:T(8,128)}, f32[128,128]{1,0:T(8,128)}) custom-call(f32[56,128,128]{2,1,0:T(8,128)} %get-tuple-element.6.state_ref, f32[128,128]{1,0:T(8,128)} %spread_input.1, f32[4,56,128]{2,1,0:T(8,128)} %get-tuple-element.7.halo_input), custom_call_target="tpu_custom_call" | custom-call | tf_op jit(solution)/shard_map/transport/pallas_call | solution.py:549
where the time goes:
time: 54.7 us; the launch traced here: 54.6 us
  Pallas kernels  54 us (99%)
  between operations  0.64 us (1%)
    pallas_call x1, Pallas kernels, per_device(): pl.pallas_call(chemistry_kernel, out_shape=(jax.ShapeDtypeStruct((FIELD_R...  48.5 us
    pallas_call x1, Pallas kernels, per_device(): pl.pallas_call(transport_kernel, out_shape=(jax.ShapeDtypeStruct((species...  5.43 us

commit v1 on v0

--- a/solution.py
+++ b/solution.py
@@ -13,7 +13,7 @@
 
 TILE = 8
 CHUNK = 16
-AHEAD = 4
+AHEAD = 3
 SLOTS = 64
 FIELD_ROWS = 56
 BLOCK = 6
@@ -291,13 +291,12 @@
 
     for tile in range(share):
         fetch(tile).wait()
-    collect(0)
     edges[DOWN] = flat[row_of(0, 0)]
     load(chunk_of(0), fields_a, operand_a)
     fields_b[...] = jnp.ones_like(fields_b)
     net_b[...] = jnp.zeros_like(net_b)
     pairs = chunks // 2
-    gathered = chunks // AHEAD
+    gathered = -(-chunks // AHEAD)
 
     @pl.loop(0, pairs)
     def _(pair):
@@ -314,7 +313,7 @@
             def _(tile):
                 fetch(tile).wait()
 
-        @pl.when(pair == gathered + 1)
+        @pl.when(pair == gathered)
         def _():
             edges[RIGHT] = sides[0]
             edges[LEFT] = sides[1]
@@ -331,10 +330,6 @@
         def _():
             leave(b - 4)
 
-        collects = (pair > 0) & (pair <= gathered)
-        for index in range(AHEAD):
-            collect(jnp.where(collects, (pair - 1) * AHEAD + 1 + index, chunks))
-
         for substep in range(SUBSTEPS):
             rates(operand_a, net_a)
             if substep == 0:
@@ -342,6 +337,7 @@
                 load(chunk_of(b), fields_b, operand_b)
             else:
                 renew(net_b, fields_b, operand_b)
+                collect(jnp.minimum(pair * AHEAD + substep - 1, chunks))
             rates(operand_b, net_b)
             if substep == SUBSTEPS - 1:
                 finish(a, *advance(net_a, fields_a))

time: 54.7 us -> 53 us (0.969)
  Pallas kernels: 54 us -> 52.2 us
    pallas_call x1, Pallas kernels: 48.5 us -> 46.8 us  [per_device(): pl.pallas_call(chemistry_kernel, out_shape=(jax.ShapeDtypeStruct((FIELD_R...]
where the time goes in v1:
time: 53 us; the launch traced here: 52.9 us
  Pallas kernels  52.2 us (98%)
  between operations  0.64 us (1%)
    pallas_call x1, Pallas kernels, per_device(): pl.pallas_call(chemistry_kernel, out_shape=(jax.ShapeDtypeStruct((FIELD_R...  46.8 us
    pallas_call x1, Pallas kernels, per_device(): pl.pallas_call(transport_kernel, out_shape=(jax.ShapeDtypeStruct((species...  5.43 us

profile of v1, /device:TPU:0, one launch (start us, length us, event | category | flops | bytes accessed | tf_op | source)
XLA Modules:
  0.0 52.9 jit_solution(5423834324895280306)
XLA Ops:
  0.6 46.8 %chemistry.1 = (f32[56,128,128]{2,1,0:T(8,128)}, f32[4,56,128]{2,1,0:T(8,128)}) custom-call(f32[53,128,128]{2,1,0:T(8,128)} %bitcast.5, f32[128,128]{1,0:T(8,128)} %temper_ref.1, f32[128,128]{1,0:T(8,128)} %spread_input.1, s32[1,128]{1,0:T(1,128)} %bitcast.8, s32[53,325]{1,0:T(8,128)} %bitcast.6, s32[53,325]{1,0:T(8,128)} %bitcast.7, f32[325]{0:T(512)} %prefactor_input.1, ...), custom_call_target="tpu_custom_call" | custom-call | tf_op jit(solution)/shard_map/chemistry/pallas_call | solution.py:489
  47.4 5.4 %transport.1 = (f32[53,128,128]{2,1,0:T(8,128)}, f32[128,128]{1,0:T(8,128)}) custom-call(f32[56,128,128]{2,1,0:T(8,128)} %get-tuple-element.6.state_ref, f32[128,128]{1,0:T(8,128)} %spread_input.1, f32[4,56,128]{2,1,0:T(8,128)} %get-tuple-element.7.halo_input), custom_call_target="tpu_custom_call" | custom-call | tf_op jit(solution)/shard_map/transport/pallas_call | solution.py:545
